TPU v7x, 512 devices: a whole 4x8x8 slice. The times are simulated.
512 devices in a mesh: ctx: 64 (over y, z), head: 8 (over x, core).
Axes of the slice: x: 4, y: 8, z: 8, core: 2. Of those that a mesh axis runs over, the one named last changes fastest.
Arguments:
- hidden_in: bfloat16 [32768, 8192], P('ctx', 'head'), may hold values from -6 to 6
- query: bfloat16 [32768, 8192], P('ctx', 'head'), may hold values from -6 to 6
- key: bfloat16 [32768, 1024], P('ctx', 'head'), may hold values from -6 to 6
- value: bfloat16 [32768, 1024], P('ctx', 'head'), may hold values from -6 to 6
- output_gradient: bfloat16 [32768, 8192], P('ctx', 'head'), may hold values from -6 to 6
- adapter_down: bfloat16 [48, 8192], P(None, 'head'), may hold values from -0.0625 to 0.0625
- up_query: bfloat16 [16, 8192], P(None, 'head'), may hold values from -0.0625 to 0.0625
- key_value_up_weight: bfloat16 [32, 1024], P(None, 'head'), may hold values from -0.1875 to 0.1875
Outputs:
- grad_query: bfloat16 [32768, 8192], P('ctx', 'head')
- key_gradient: bfloat16 [32768, 1024], P('ctx', 'head')
- value_gradient: bfloat16 [32768, 1024], P('ctx', 'head')
- grad_down: float32 [48, 8192], P(None, 'head')
- grad_up_query: float32 [16, 8192], P(None, 'head')
- grad_up_kv: float32 [32, 1024], P(None, 'head')
All inputs are finite; a program needn't handle non-finite values.
Results may differ from a plain program's by a relative error of at most 0.014.
Values may be sent and summed in bfloat16 or wider, within the bound.
No kernel may reach another device: no remote copies, remote signals or barrier semaphores. Data moves between devices by JAX's collectives and lax.ppermute only.
A program may use at most 64 MiB of HBM per device.

v0:
```python
import math

import jax
import jax.numpy as jnp
from jax import lax
from jax.sharding import PartitionSpec as P

QUERY_HEADS = 64
KEY_VALUE_HEADS = 8
HEAD_WIDTH = 128
ADAPTER_RANK = 16


def copy_for_each(array, axis):
    copies = jnp.broadcast_to(array, (lax.axis_size(axis), *array.shape))
    return lax.all_to_all(copies, axis, split_axis=0, concat_axis=0, tiled=True)


def over_copies(array, axis):
    everything = copy_for_each(array, axis)
    return jnp.sum(everything.astype(jnp.float32), axis=0)


def filled_up(lines, peers):
    spare = -len(lines) % peers
    return jnp.pad(lines, [(0, spare)] + [(0, 0)] * (lines.ndim - 1))


def in_order(blocks, dim):
    blocks = jnp.moveaxis(blocks, 0, dim)
    shape = blocks.shape
    return blocks.reshape(*shape[:dim], shape[dim] * shape[dim + 1], *shape[dim + 2 :])


def gathered_copies(array, axis, dim):
    return in_order(copy_for_each(array, axis), dim)


def in_blocks(array, dim, peers):
    before, after = (array.shape[:dim], array.shape[dim + 1 :])
    return jnp.moveaxis(array.reshape(*before, peers, -1, *after), dim, 0)


def sent_and_summed(array, axis, dim):
    peers = lax.axis_size(axis)
    blocks = lax.all_to_all(in_blocks(array, dim, peers), axis, 0, 0, tiled=True)
    return jnp.sum(blocks, axis=0)


def nested_sum(array, axes):
    padded = filled_up(array, lax.axis_size(axes))
    whole = gathered_copies(sent_and_summed(padded, axes, 0), axes, 0)
    return lax.slice_in_dim(whole, 0, len(array)).reshape(array.shape)


def together(arrays, axis):
    ends = [0]
    for a in arrays:
        ends.append(ends[-1] + a.size)
    so_far = nested_sum(jnp.concatenate([a.ravel() for a in arrays]), axis)
    return tuple((so_far[b:e].reshape(a.shape) for a, b, e in zip(arrays, ends, ends[1:])))


def contract_rows(left, right):
    return lax.dot_general(
        left, right, (((0,), (0,)), ((), ())), preferred_element_type=jnp.float32
    )


def project_back(rows, weights):
    return lax.dot_general(
        rows, weights, (((1,), (1,)), ((), ())), preferred_element_type=jnp.float32
    )


def on_device(
    hidden_in, query, key, value, output_gradient, adapter_down, up_query, key_value_up_weight
):
    rows_here = hidden_in.shape[0]
    ctx_count = lax.axis_size("ctx")
    total_tokens = rows_here * ctx_count
    query_group_width = QUERY_HEADS // KEY_VALUE_HEADS
    kv_local = key.shape[1] // HEAD_WIDTH
    att_scale = 1.0 / math.sqrt(HEAD_WIDTH * total_tokens)
    grad_scale = 1.0 / math.sqrt(total_tokens)
    rows_of_queries = query.reshape(rows_here, kv_local, query_group_width, HEAD_WIDTH)
    gradient_rows = output_gradient.reshape(rows_here, kv_local, query_group_width, HEAD_WIDTH)
    rows_of_keys = key.reshape(rows_here, kv_local, HEAD_WIDTH)
    rows_of_values = value.reshape(rows_here, kv_local, HEAD_WIDTH)
    state_kv = jnp.einsum(
        "sjd,sje->jde", rows_of_keys, rows_of_values, preferred_element_type=jnp.float32
    )
    state_qo = jnp.einsum(
        "tjgd,tjge->jde", rows_of_queries, gradient_rows, preferred_element_type=jnp.float32
    )
    stacked = jnp.stack([state_kv, state_qo])[None]
    gathered = lax.all_gather(stacked, "ctx", axis=0, tiled=True)
    my_index = lax.axis_index("ctx")
    positions = jnp.arange(ctx_count, dtype=jnp.int32)
    before = (positions < my_index).astype(jnp.float32)
    after = (positions > my_index).astype(jnp.float32)
    prefix = jnp.einsum("n,njde->jde", before, gathered[:, 0], precision=lax.Precision.HIGHEST)
    suffix = jnp.einsum("n,njde->jde", after, gathered[:, 1], precision=lax.Precision.HIGHEST)
    prefix_low = prefix.astype(jnp.bfloat16)
    suffix_low = suffix.astype(jnp.bfloat16)
    causal = jnp.arange(rows_here)[None, :] <= jnp.arange(rows_here)[:, None]
    score_do = jnp.where(
        causal,
        jnp.einsum(
            "tjgd,sjd->jgts", gradient_rows, rows_of_values, preferred_element_type=jnp.float32
        ),
        0.0,
    ).astype(jnp.bfloat16)
    score_qk = jnp.where(
        causal,
        jnp.einsum(
            "tjgd,sjd->jgts", rows_of_queries, rows_of_keys, preferred_element_type=jnp.float32
        ),
        0.0,
    ).astype(jnp.bfloat16)
    grad_q = jnp.einsum(
        "jgts,sjd->tjgd", score_do, rows_of_keys, preferred_element_type=jnp.float32
    ) + jnp.einsum("tjge,jde->tjgd", gradient_rows, prefix_low, preferred_element_type=jnp.float32)
    key_gradient_part = jnp.einsum(
        "jgts,tjgd->sjd", score_do, rows_of_queries, preferred_element_type=jnp.float32
    ) + jnp.einsum("sje,jde->sjd", rows_of_values, suffix_low, preferred_element_type=jnp.float32)
    value_gradient_part = jnp.einsum(
        "jgts,tjge->sje", score_qk, gradient_rows, preferred_element_type=jnp.float32
    ) + jnp.einsum("sjd,jde->sje", rows_of_keys, suffix_low, preferred_element_type=jnp.float32)
    grad_query = (
        (att_scale * grad_q)
        .astype(jnp.bfloat16)
        .reshape(rows_here, kv_local * query_group_width * HEAD_WIDTH)
    )
    key_gradient = (
        (att_scale * key_gradient_part)
        .astype(jnp.bfloat16)
        .reshape(rows_here, kv_local * HEAD_WIDTH)
    )
    value_gradient = (
        (att_scale * value_gradient_part)
        .astype(jnp.bfloat16)
        .reshape(rows_here, kv_local * HEAD_WIDTH)
    )
    back_part = jnp.concatenate(
        [
            project_back(grad_query, up_query),
            project_back(key_gradient, key_value_up_weight[:ADAPTER_RANK]),
            project_back(value_gradient, key_value_up_weight[ADAPTER_RANK:]),
        ],
        axis=1,
    )
    low_part = project_back(hidden_in, adapter_down)
    low_sum, back_sum = (
        over_copies(low_part.astype(jnp.bfloat16), "head").astype(jnp.float32),
        over_copies(back_part.astype(jnp.bfloat16), "head").astype(jnp.float32),
    )
    low_rows = low_sum.astype(jnp.bfloat16)
    back_rows_low = back_sum.astype(jnp.bfloat16)
    down_part = contract_rows(back_rows_low, hidden_in)
    upq_part = contract_rows(low_rows[:, :ADAPTER_RANK], grad_query)
    upkv_part = jnp.concatenate(
        [
            contract_rows(low_rows[:, ADAPTER_RANK : 2 * ADAPTER_RANK], key_gradient),
            contract_rows(low_rows[:, 2 * ADAPTER_RANK :], value_gradient),
        ],
        axis=0,
    )
    down_sum, upq_sum, upkv_sum = together((down_part, upq_part, upkv_part), "ctx")
    return (
        grad_query,
        key_gradient,
        value_gradient,
        grad_scale * down_sum,
        grad_scale * upq_sum,
        grad_scale * upkv_sum,
    )


def solution(mesh):
    placed = (
        P("ctx", "head"),
        P("ctx", "head"),
        P("ctx", "head"),
        P("ctx", "head"),
        P("ctx", "head"),
        P(None, "head"),
        P(None, "head"),
        P(None, "head"),
    )
    return jax.shard_map(
        on_device,
        mesh=mesh,
        in_specs=placed,
        out_specs=(
            P("ctx", "head"),
            P("ctx", "head"),
            P("ctx", "head"),
            P(None, "head"),
            P(None, "head"),
            P(None, "head"),
        ),
        check_vma=False,
    )
```

profile of v0, /device:TPU:2, one launch (start us, length us, event | category | flops | bytes accessed | tf_op | source)
XLA Modules:
  0.0 198.8 jit_solution(9612763807216786590)
XLA Ops:
  7.2 0.0 copy-start
  7.2 0.0 all-gather.3.cloned.1.call-start
  7.2 1.6 copy.82
  8.8 1.5 copy.83
  10.3 0.0 copy-start.4
  10.3 0.0 copy-start.5
  10.3 0.0 copy-start.10
  10.3 0.0 copy-start.2
  10.4 0.5 convolution_bitcast_fusion.3
  10.8 0.4 copy-done.4
  11.2 0.1 copy-done.5
  11.3 0.2 convolution_bitcast_fusion.4
  11.5 0.7 pad_maximum_fusion.1
  12.2 0.0 all-gather.3.cloned.1.call-update
  12.2 0.0 copy-done
  12.2 0.0 copy-done.10
  12.2 0.4 convolution_convert_fusion
  12.7 0.8 broadcast_in_dim.30
  13.4 9.3 %all-to-all-start.1 = ((bf16[8,512,48]{1,2,0:T(8,128)(2,1)}), bf16[8,512,48]{1,2,0:T(8,128)(2,1)S(1)}, u32[]{:S(2)}, u32[]{:S(2)}) async-start(bf16[8,512,48]{1,2,0:T(8,128)(2,1)} %broadcast_in_dim.30), calls=%async_computation.1 | async-start | bytes 786432 | tf_op jit(solution)/shard_map/all_to_all | solution.py:16
  22.7 0.1 iota_compare_fusion
  22.8 0.0 copy-done.2
  22.8 1.3 fusion.2
  24.1 0.0 copy-start.1
  24.1 2.0 copy-done.1
  26.1 1.2 convolution_bitcast_fusion
  27.3 4.4 %fusion.18 = f32[128,512]{0,1:T(8,128)} fusion(pred[512,512]{0,1:T(8,128)(4,1)S(1)} %iota_compare_fusion, bf16[512,128]{1,0:T(8,128)(2,1)S(1)} %copy-done.5, bf16[512,1024]{1,0:T(8,128)(2,1)} %param.9, bf16[512,1024]{1,0:T(8,128)(2,1)S(1)} %copy-done.2), kind=kOutput, calls=%fused_computation.24 | convolution fusion | flops 1077936128 | bytes 2752512 | tf_op jit(solution)/shard_map/jgts,tjge->sje/dot_general | solution.py:127
  31.7 4.4 %fusion.39 = f32[8,512,128]{1,2,0:T(8,128)} fusion(bf16[8,512,512]{1,2,0:T(8,128)(2,1)} %copy-done.1, bf16[512,128]{1,0:T(8,128)(2,1)S(1)} %copy-done.5), kind=kOutput, calls=%fused_computation.52 | convolution fusion | flops 536870912 | bytes 6422528 | tf_op jit(solution)/shard_map/jgts,sjd->tjgd/dot_general | solution.py:121
  36.1 0.0 all-to-all-done.1
  36.1 0.1 reduce_sum.34
  36.2 80.2 %all-gather.3.cloned.1.call-done = f32[128,1,128,128]{3,2,1,0:T(8,128)} async-done(((f32[2,1,128,128]{3,2,1,0:T(8,128)}), f32[128,1,128,128]{3,2,1,0:T(8,128)}) %all-gather.3.cloned.1.call-update) | async-done | bytes 8388624 | tf_op jit(solution)/shard_map/all_gather | solution.py:97
  116.4 4.1 %slice_bitcast_fusion = (f32[64,128,128]{2,1,0:T(8,128)S(1)}, f32[64,128,128]{2,1,0:T(8,128)S(1)}) fusion(f32[64,2,1,128,128]{4,3,1,0,2:T(8,128)} %bitcast.161), kind=kLoop, calls=%fused_computation.7 | loop fusion | bytes 16777216 | tf_op jit(solution)/shard_map/reshape.43
  120.4 0.0 copy-start.12
  120.5 3.8 %fusion.6 = f32[1,128,128]{2,0,1:T(1,128)S(1)} fusion(f32[64,128,128]{2,1,0:T(8,128)S(1)} %get-tuple-element.36, s32[]{:T(128)S(6)} %axis_index.15), kind=kOutput, calls=%fused_computation.9 | convolution fusion | flops 12582976 | bytes 4259844 | tf_op jit(solution)/shard_map/n,njde->jde/dot_general | solution.py:103
  124.3 4.0 %fusion.8 = f32[1,128,128]{2,0,1:T(1,128)S(1)} fusion(f32[64,128,128]{2,1,0:T(8,128)S(1)} %get-tuple-element.37, s32[]{:T(128)S(6)} %axis_index.15), kind=kOutput, calls=%fused_computation.11 | convolution fusion | flops 12582976 | bytes 4259844 | tf_op jit(solution)/shard_map/n,njde->jde/dot_general | solution.py:102
  128.3 0.2 fusion.24
  128.5 0.0 copy-start.6
  128.5 0.2 fusion.23
  128.7 0.0 copy-start.7
  128.7 0.1 convolution_convert_fusion.3
  128.8 0.2 convolution_convert_fusion.2
  129.0 0.5 fusion.15
  129.5 0.0 copy-done.11
  129.5 0.2 convolution_convert_fusion.1
  129.7 0.8 broadcast_in_dim.29
  130.5 4.8 %all-to-all-start = ((bf16[8,512,48]{1,2,0:T(8,128)(2,1)}), bf16[8,512,48]{1,2,0:T(8,128)(2,1)S(1)}, u32[]{:S(2)}, u32[]{:S(2)}) async-start(bf16[8,512,48]{1,2,0:T(8,128)(2,1)} %broadcast_in_dim.29), calls=%async_computation | async-start | bytes 786432 | tf_op jit(solution)/shard_map/all_to_all | solution.py:16
  135.3 0.1 fusion.46
  135.5 0.4 convolution_bitcast_fusion.2
  135.9 0.1 fusion.44
  136.0 6.8 %all-to-all-done = bf16[8,512,48]{1,2,0:T(8,128)(2,1)S(1)} async-done(((bf16[8,512,48]{1,2,0:T(8,128)(2,1)}), bf16[8,512,48]{1,2,0:T(8,128)(2,1)S(1)}, u32[]{:S(2)}, u32[]{:S(2)}) %all-to-all-start) | async-done | bytes 393248 | tf_op jit(solution)/shard_map/all_to_all | solution.py:16
  142.8 0.1 reduce_sum.33
  142.9 0.3 convolution_bitcast_fusion.1
  143.3 0.4 all_to_all.18
  143.6 25.2 %all_to_all.25 = f32[64,1,1088]{2,1,0:T(1,128)S(1)} all-to-all(f32[64,1,1088]{2,1,0:T(1,128)S(1)} %all_to_all.18), channel_id=1, replica_groups=mesh['ctx'=64,'head'=8] {'ctx'}, dimensions={0} | all-to-all | bytes 557056 | tf_op jit(solution)/shard_map/all_to_all | solution.py:46
  168.8 0.2 reduce_sum.35
  169.0 0.9 broadcast_in_dim.31
  169.9 4.6 %all-to-all-start.3 = ((f32[64,1,1088]{2,1,0:T(1,128)}), f32[64,1,1088]{2,1,0:T(1,128)S(1)}, u32[]{:S(2)}, u32[]{:S(2)}) async-start(f32[64,1,1088]{2,1,0:T(1,128)} %broadcast_in_dim.31), calls=%async_computation.3 | async-start | bytes 589824 | tf_op jit(solution)/shard_map/all_to_all | solution.py:16
  174.5 1.3 copy.69
  175.8 13.2 %all-to-all-done.3 = f32[64,1,1088]{2,1,0:T(1,128)S(1)} async-done(((f32[64,1,1088]{2,1,0:T(1,128)}), f32[64,1,1088]{2,1,0:T(1,128)S(1)}, u32[]{:S(2)}, u32[]{:S(2)}) %all-to-all-start.3) | async-done | bytes 278560 | tf_op jit(solution)/shard_map/all_to_all | solution.py:16
  189.0 0.7 reduce.3
  189.7 0.2 slice.44
  189.9 0.7 slice_multiply_fusion
  190.6 0.6 slice_multiply_fusion.1
  191.2 0.1 slice.47
  191.4 0.6 slice_multiply_fusion.2
  (15 shorter events, 0.1 us)
Async XLA Ops:
  7.2 5.0 %copy-start = (bf16[512,1024]{1,0:T(8,128)(2,1)S(1)}, bf16[512,1024]{1,0:T(8,128)(2,1)}, u32[]{:S(2)}) copy-start(bf16[512,1024]{1,0:T(8,128)(2,1)} %param.8) | copy-start | bytes 3145732
  7.2 109.2 %all-gather.3.cloned.1.call-start = ((), (), s32[]{:S(2)}) async-start(), calls=%async_computation.4 | async-start | bytes 8519680 | tf_op jit(solution)/shard_map/all_gather | solution.py:97
  10.3 0.9 copy-start.4
  10.3 1.0 copy-start.5
  10.3 1.9 copy-start.10
  10.3 12.4 %copy-start.2 = (bf16[512,1024]{1,0:T(8,128)(2,1)S(1)}, bf16[512,1024]{1,0:T(8,128)(2,1)}, u32[]{:S(2)}) copy-start(bf16[512,1024]{1,0:T(8,128)(2,1)} %param.12) | copy-start | bytes 3145732
  13.4 22.7 %all-to-all-start.1 = ((bf16[8,512,48]{1,2,0:T(8,128)(2,1)}), bf16[8,512,48]{1,2,0:T(8,128)(2,1)S(1)}, u32[]{:S(2)}, u32[]{:S(2)}) async-start(bf16[8,512,48]{1,2,0:T(8,128)(2,1)} %broadcast_in_dim.30), calls=%async_computation.1 | async-start | bytes 786432 | tf_op jit(solution)/shard_map/all_to_all | solution.py:16
  22.7 3.4 %copy-start.8 = (bf16[512,1024]{1,0:T(8,128)(2,1)S(1)}, bf16[512,1024]{1,0:T(8,128)(2,1)}, u32[]{:S(2)}) copy-start(bf16[512,1024]{1,0:T(8,128)(2,1)} %param.9) | copy-start | bytes 3145732
  24.1 2.0 copy-start.1
  120.4 8.0 %copy-start.9 = (f32[128,512]{0,1:T(8,128)S(1)}, f32[128,512]{0,1:T(8,128)}, u32[]{:S(2)}) copy-start(f32[128,512]{0,1:T(8,128)} %fusion.18) | copy-start | bytes 786436
  120.4 8.2 %copy-start.12 = (bf16[32,128]{1,0:T(8,128)(2,1)S(1)}, bf16[32,128]{1,0:T(8,128)(2,1)}, u32[]{:S(2)}) copy-start(bf16[32,128]{1,0:T(8,128)(2,1)} %param.15) | copy-start | bytes 24580
  120.4 8.5 %copy-start.3 = (f32[8,512,128]{1,2,0:T(8,128)S(1)}, f32[8,512,128]{1,2,0:T(8,128)}, u32[]{:S(2)}) copy-start(f32[8,512,128]{1,2,0:T(8,128)} %fusion.39) | copy-start | bytes 6291460
  124.3 5.2 %copy-start.11 = (bf16[16,1024]{1,0:T(8,128)(2,1)S(1)}, bf16[16,1024]{1,0:T(8,128)(2,1)}, u32[]{:S(2)}) copy-start(bf16[16,1024]{1,0:T(8,128)(2,1)} %param.14) | copy-start | bytes 98308
  128.5 7.4 %copy-start.6 = (bf16[512,128]{1,0:T(8,128)(2,1)}, bf16[512,128]{1,0:T(8,128)(2,1)S(1)}, u32[]{:S(2)}) copy-start(bf16[512,128]{1,0:T(8,128)(2,1)S(1)} %fusion.24) | copy-start | bytes 393220
  128.7 7.2 %copy-start.7 = (bf16[512,128]{1,0:T(8,128)(2,1)}, bf16[512,128]{1,0:T(8,128)(2,1)S(1)}, u32[]{:S(2)}) copy-start(bf16[512,128]{1,0:T(8,128)(2,1)S(1)} %fusion.23) | copy-start | bytes 393220
  130.5 12.3 %all-to-all-start = ((bf16[8,512,48]{1,2,0:T(8,128)(2,1)}), bf16[8,512,48]{1,2,0:T(8,128)(2,1)S(1)}, u32[]{:S(2)}, u32[]{:S(2)}) async-start(bf16[8,512,48]{1,2,0:T(8,128)(2,1)} %broadcast_in_dim.29), calls=%async_computation | async-start | bytes 786432 | tf_op jit(solution)/shard_map/all_to_all | solution.py:16
  169.9 19.1 %all-to-all-start.3 = ((f32[64,1,1088]{2,1,0:T(1,128)}), f32[64,1,1088]{2,1,0:T(1,128)S(1)}, u32[]{:S(2)}, u32[]{:S(2)}) async-start(f32[64,1,1088]{2,1,0:T(1,128)} %broadcast_in_dim.31), calls=%async_computation.3 | async-start | bytes 589824 | tf_op jit(solution)/shard_map/all_to_all | solution.py:16
Sparse Core Ops, SparseCore 0:
  12.3 103.9 all-gather.2
where the time goes:
time: 199 us
  waiting for transfers between devices  100 us (50%)
  blocking collectives  25.2 us (13%)
  matrix products  22.5 us (11%)
  starting transfers between devices  18.7 us (9%)
  between operations  14.3 us (7%)
  local copies, waits for them, and re-layouts  14.1 us (7%)
  other arithmetic  3.74 us (2%)
    all_gather x1, waiting for transfers between devices, on_device(): gathered = lax.all_gather(stacked, 'ctx', axis=0, tiled=True)  80.2 us
    all_to_all x1, blocking collectives, sent_and_summed(): lax.all_to_all(in_blocks(array, dim, peers), axis, 0, 0, tiled=True)  25.2 us
    all_to_all x3, waiting for transfers between devices, copy_for_each(): return lax.all_to_all(copies, axis, split_axis=0, concat_axis=0, tiled=True)  19.9 us
    all_to_all x3, starting transfers between devices, copy_for_each(): return lax.all_to_all(copies, axis, split_axis=0, concat_axis=0, tiled=True)  18.7 us
    unnamed x31, local copies, waits for them, and re-layouts  6.92 us
    dot_general x1, matrix products, on_device(): jnp.einsum('jgts,tjge->sje', score_qk, gradient_rows, preferred_element_t...  4.39 us
    dot_general x1, matrix products, on_device(): jnp.einsum('jgts,sjd->tjgd', score_do, rows_of_keys, preferred_element_ty...  4.38 us
    another operation x1, local copies, waits for them, and re-layouts  4.06 us
  transfers between devices with their start and end apart: 4, of which 3 were waited for; matrix products, arithmetic and copies ran while one was open for 7% of the time, Pallas kernels for 0%

commit v1 on v0

v1 whole, which is shorter than its diff:
```python
import functools
import math

import jax
import jax.numpy as jnp
from jax import lax
from jax.experimental import pallas as pl
from jax.experimental.pallas import tpu as pltpu
from jax.sharding import Mesh
from jax.sharding import PartitionSpec as P

HEAD_WIDTH = 128
ADAPTER_RANK = 16
RINGS = 8
GRAD_ROWS = 10
MIB = 1024 * 1024
ALONE = 63

F32 = jnp.float32
BF16 = jnp.bfloat16


def params(mebibytes=16):
    return pltpu.CompilerParams(vmem_limit_bytes=mebibytes * MIB)


def nn(a, b):
    return lax.dot_general(a, b, (((1,), (0,)), ((), ())), preferred_element_type=F32)


def nt(a, b):
    return lax.dot_general(a, b, (((1,), (1,)), ((), ())), preferred_element_type=F32)


def tn(a, b):
    return lax.dot_general(a, b, (((0,), (0,)), ((), ())), preferred_element_type=F32)


def grid2(rows, columns):
    return (
        lax.broadcasted_iota(jnp.int32, (rows, columns), 0),
        lax.broadcasted_iota(jnp.int32, (rows, columns), 1),
    )


def ones_where(mask):
    return jnp.where(mask, 1.0, 0.0).astype(BF16)


def states_kernel(
    q_ref, d_ref, k_ref, v_ref, out_ref, chunk_ref, q_buf, d_buf, k_buf, v_buf, sems
):
    tokens, width = q_ref.shape
    half = tokens // 2
    copies = [
        pltpu.make_async_copy(k_ref, k_buf, sems.at[0]),
        pltpu.make_async_copy(v_ref, v_buf, sems.at[1]),
    ]
    for i in range(2):
        at = pl.ds(i * half, half)
        copies += [
            pltpu.make_async_copy(q_ref.at[at], q_buf.at[at], sems.at[2 + 2 * i]),
            pltpu.make_async_copy(d_ref.at[at], d_buf.at[at], sems.at[3 + 2 * i]),
        ]
    for copy in copies:
        copy.start()
    state_kv, state_qo = [], []
    copies[0].wait()
    copies[1].wait()
    for i in range(2):
        rows = pl.ds(i * half, half)
        state_kv.append(tn(k_buf[rows, :], v_buf[rows, :]))
    for i in range(2):
        rows = pl.ds(i * half, half)
        copies[2 + 2 * i].wait()
        copies[3 + 2 * i].wait()
        total = jnp.zeros((HEAD_WIDTH, HEAD_WIDTH), F32)
        for h in range(width // HEAD_WIDTH):
            at = pl.ds(h * HEAD_WIDTH, HEAD_WIDTH)
            total += tn(q_buf[rows, at], d_buf[rows, at])
        state_qo.append(total)
    peers, rows, _ = out_ref.shape
    rows //= 2
    whole_kv = (state_kv[0] + state_kv[1]).astype(BF16)
    whole_qo = (state_qo[0] + state_qo[1]).astype(BF16)
    for i in range(peers):
        part = slice(i * rows, (i + 1) * rows)
        out_ref[i, pl.ds(0, rows), :] = whole_kv[part]
        out_ref[i, pl.ds(rows, rows), :] = whole_qo[part]
    chunk_ref[pl.ds(0, HEAD_WIDTH), :] = state_kv[0].astype(BF16)
    chunk_ref[pl.ds(HEAD_WIDTH, HEAD_WIDTH), :] = state_qo[1].astype(BF16)


def scan_kernel(x_ref, out_ref, token_ref):
    size, rows, _ = x_ref.shape
    rows //= 2
    ring = lax.axis_index("ring")
    kv = [x_ref[i, pl.ds(0, rows), :].astype(F32) for i in range(size)]
    qo = [x_ref[i, pl.ds(rows, rows), :].astype(F32) for i in range(size)]
    nothing = jnp.zeros_like(kv[0])
    before, after = [nothing], [nothing]
    for i in range(size):
        before.append(before[-1] + kv[i])
        after.append(after[-1] + qo[size - 1 - i])
    for there in range(out_ref.shape[0] // size):
        for i in range(size):
            kv_part = jnp.where(
                ring < there, before[size], jnp.where(ring == there, before[i], nothing)
            )
            qo_part = jnp.where(
                ring > there, after[size], jnp.where(ring == there, after[size - 1 - i], nothing)
            )
            out_ref[there * size + i, pl.ds(0, rows), :] = kv_part.astype(BF16)
            out_ref[there * size + i, pl.ds(rows, rows), :] = qo_part.astype(BF16)
    token_ref[...] = jnp.zeros_like(token_ref)


def local_kernel(
    q_ref, d_ref, k_ref, v_ref, chunk_ref, after_ref, gq_ref, kg_ref, vg_ref, kv_ref
):
    tokens, width = q_ref.shape
    half = tokens // 2
    row, column = grid2(half, half)
    causal = column <= row

    def masked(scores):
        return jnp.where(causal, scores, 0.0).astype(BF16)

    kv_ref[:, pl.ds(0, HEAD_WIDTH)] = k_ref[...]
    kv_ref[:, pl.ds(HEAD_WIDTH, HEAD_WIDTH)] = v_ref[...]
    state_kv = chunk_ref[pl.ds(0, HEAD_WIDTH), :]
    state_qo = chunk_ref[pl.ds(HEAD_WIDTH, HEAD_WIDTH), :]
    for i in range(2):
        rows = pl.ds(i * half, half)
        k, v = k_ref[rows, :], v_ref[rows, :]
        if i == 0:
            key_gradient, value_gradient = nt(v, state_qo), nn(k, state_qo)
        else:
            key_gradient = value_gradient = jnp.zeros((half, HEAD_WIDTH), F32)
        for h in range(width // HEAD_WIDTH):
            at = pl.ds(h * HEAD_WIDTH, HEAD_WIDTH)
            q, d = q_ref[rows, at], d_ref[rows, at]
            score_do = masked(nt(d, v))
            score_qk = masked(nt(q, k))
            grad_query = nn(score_do, k)
            if i == 1:
                grad_query += nt(d, state_kv)
            gq_ref[rows, at] = grad_query.astype(BF16)
            key_gradient += tn(score_do, q)
            value_gradient += tn(score_qk, d)
        kg_ref[rows, :] = key_gradient
        vg_ref[rows, :] = value_gradient


def low_kernel(hidden_ref, down_ref, after_ref, out_ref):
    out_ref[...] = nt(down_ref[...], hidden_ref[...]).astype(BF16)


def grads_kernel(
    scale, state_ref, gq_ref, kgl_ref, vgl_ref, d_ref, kv_ref, up_ref, kvup_ref, low_ref,
    query_ref, key_ref, value_ref, send_ref,
):
    tokens, width = d_ref.shape
    rank = low_ref.shape[0]
    size = state_ref.shape[0] // RINGS
    state_rows = state_ref.shape[1] // 2
    prefix, suffix = [], []
    for i in range(size):
        total = sum(state_ref[ring * size + i].astype(F32) for ring in range(RINGS))
        prefix.append(total[:state_rows])
        suffix.append(total[state_rows:])
    prefix = jnp.concatenate(prefix, axis=0).astype(BF16)
    suffix = jnp.concatenate(suffix, axis=0).astype(BF16)
    k, v = kv_ref[:, pl.ds(0, HEAD_WIDTH)], kv_ref[:, pl.ds(HEAD_WIDTH, HEAD_WIDTH)]
    key_gradient = (scale * (kgl_ref[...] + nt(v, suffix))).astype(BF16)
    value_gradient = (scale * (vgl_ref[...] + nn(k, suffix))).astype(BF16)
    key_ref[...] = key_gradient
    value_ref[...] = value_gradient
    back = jnp.zeros((ADAPTER_RANK, tokens), F32)
    for h in range(width // HEAD_WIDTH):
        at = pl.ds(h * HEAD_WIDTH, HEAD_WIDTH)
        grad_query = gq_ref[:, at].astype(F32) + nt(d_ref[:, at], prefix)
        grad_query = (scale * grad_query).astype(BF16)
        query_ref[:, at] = grad_query
        back += nt(up_ref[:, at], grad_query)
    whole = jnp.concatenate(
        [
            back,
            nt(kvup_ref[pl.ds(0, ADAPTER_RANK), :], key_gradient),
            nt(kvup_ref[pl.ds(ADAPTER_RANK, ADAPTER_RANK), :], value_gradient),
        ],
        axis=0,
    ).astype(BF16)
    for i in range(send_ref.shape[0]):
        send_ref[i, pl.ds(0, rank), :] = whole
        send_ref[i, pl.ds(rank, rank), :] = low_ref[...]


def down_kernel(parts_ref, hidden_ref, query_ref, key_ref, value_ref, out_ref):
    peers, rows, _ = parts_ref.shape
    rank = rows // 2
    heads = hidden_ref.shape[1] // HEAD_WIDTH
    both = sum(parts_ref[i].astype(F32) for i in range(peers)).astype(BF16)
    back, low = both[:rank], both[rank:]
    down = nn(back, hidden_ref[...]).astype(BF16)
    up_query = nn(low[:ADAPTER_RANK], query_ref[...]).astype(BF16)
    at = heads * rank
    for i in range(heads):
        part = slice(i * HEAD_WIDTH, (i + 1) * HEAD_WIDTH)
        out_ref[pl.ds(i * rank, rank), :] = down[:, part]
        out_ref[pl.ds(at + i * ADAPTER_RANK, ADAPTER_RANK), :] = up_query[:, part]
    at += heads * ADAPTER_RANK
    out_ref[pl.ds(at, ADAPTER_RANK), :] = nn(
        low[ADAPTER_RANK : 2 * ADAPTER_RANK], key_ref[...]
    ).astype(BF16)
    at += ADAPTER_RANK
    out_ref[pl.ds(at, ADAPTER_RANK), :] = nn(
        low[2 * ADAPTER_RANK :], value_ref[...]
    ).astype(BF16)
    at += ADAPTER_RANK
    out_ref[pl.ds(at, out_ref.shape[0] - at), :] = jnp.zeros(
        (out_ref.shape[0] - at, HEAD_WIDTH), BF16
    )


def sum_kernel(x_ref, out_ref):
    rows = x_ref.shape[0]
    row, column = grid2(16, rows)
    total = nn(ones_where(lax.rem(column, GRAD_ROWS) == row), x_ref[...]).astype(BF16)
    row, column = grid2(rows, 16)
    out_ref[...] = nn(ones_where(lax.rem(row, GRAD_ROWS) == column), total).astype(BF16)


def finish_kernel(scale, x_ref, down_ref, query_ref, kv_ref):
    rank = down_ref.shape[0]
    parts = down_ref.shape[1] // HEAD_WIDTH
    for i in range(parts):
        at = pl.ds(i * HEAD_WIDTH, HEAD_WIDTH)
        down_ref[:, at] = scale * x_ref[pl.ds(i * rank, rank), :].astype(F32)
    start = parts * rank
    for i in range(parts):
        at = pl.ds(i * HEAD_WIDTH, HEAD_WIDTH)
        query_ref[:, at] = scale * x_ref[
            pl.ds(start + i * ADAPTER_RANK, ADAPTER_RANK), :
        ].astype(F32)
    start += parts * ADAPTER_RANK
    kv_ref[...] = scale * x_ref[pl.ds(start, 2 * ADAPTER_RANK), :].astype(F32)


def shape(dims, dtype):
    return jax.ShapeDtypeStruct(dims, dtype)


def call(kernel, out_shape, flops, nbytes, name, mebibytes=16, **more):
    return pl.pallas_call(
        kernel,
        out_shape=out_shape,
        compiler_params=params(mebibytes),
        cost_estimate=pl.CostEstimate(flops=flops, bytes_accessed=nbytes, transcendentals=0),
        name=name,
        **more,
    )


def exchange(blocks, axis):
    return lax.all_to_all(blocks, axis, split_axis=0, concat_axis=0, tiled=True)


def on_device(hidden, query, key, value, d_out, down, up_query, kv_up):
    tokens, width = query.shape
    heads = width // HEAD_WIDTH
    ctx_axes = ("ring", "place")
    ctx, size, peers = (lax.axis_size(axis) for axis in (ctx_axes, "place", "head"))
    ranks = down.shape[0]
    att_scale = 1.0 / math.sqrt(HEAD_WIDTH * tokens * ctx)
    grad_scale = 1.0 / math.sqrt(tokens * ctx)
    state_rows = 2 * HEAD_WIDTH // size

    block = (tokens, HEAD_WIDTH)
    hbm = pl.BlockSpec(memory_space=pltpu.HBM)
    sent, chunk = pl.pallas_call(
        states_kernel,
        in_specs=[hbm] * 4,
        out_shape=[
            shape((size, state_rows, HEAD_WIDTH), BF16),
            shape((2 * HEAD_WIDTH, HEAD_WIDTH), BF16),
        ],
        scratch_shapes=[
            pltpu.VMEM((tokens, width), BF16),
            pltpu.VMEM((tokens, width), BF16),
            pltpu.VMEM(block, BF16),
            pltpu.VMEM(block, BF16),
            pltpu.SemaphoreType.DMA((6,)),
        ],
        compiler_params=params(ALONE),
        cost_estimate=pl.CostEstimate(
            flops=10**8, bytes_accessed=2 * 10**6, transcendentals=0
        ),
        name="states",
    )(query, d_out, key, value)
    ring_states = exchange(sent, "place")

    vmem, anywhere = (pl.BlockSpec(memory_space=space) for space in (pltpu.VMEM, pl.ANY))
    low = call(
        low_kernel,
        shape((ranks, tokens), BF16),
        10**8,
        2 * 10**6,
        "low",
        ALONE,
        in_specs=[vmem, vmem, anywhere],
    )(hidden, down, chunk)

    scanned, token = call(
        scan_kernel,
        [shape((ctx, state_rows, HEAD_WIDTH), BF16), shape((8, HEAD_WIDTH), F32)],
        10**6,
        6 * 10**5,
        "scan",
    )(ring_states)
    around = exchange(scanned, ctx_axes)
    local_q, local_k, local_v, key_value = call(
        local_kernel,
        [
            shape((tokens, width), BF16),
            shape(block, F32),
            shape(block, F32),
            shape((tokens, 2 * HEAD_WIDTH), BF16),
        ],
        2 * 10**9,
        5 * 10**6,
        "local",
    )(query, d_out, key, value, chunk, token)

    grad_query, key_gradient, value_gradient, copies = call(
        functools.partial(grads_kernel, att_scale),
        [
            shape((tokens, width), BF16),
            shape(block, BF16),
            shape(block, BF16),
            shape((peers, 2 * ranks, tokens), BF16),
        ],
        2 * 10**8,
        5 * 10**6,
        "grads",
    )(
        around, local_q, local_k, local_v, d_out, key_value, up_query, kv_up, low
    )
    both_parts = exchange(copies, "head")
    rows = ctx * GRAD_ROWS
    partial = call(down_kernel, shape((rows, HEAD_WIDTH), BF16), 5 * 10**7, 2 * 10**6, "down")(
        both_parts, hidden, grad_query, key_gradient, value_gradient
    )
    split = (ctx, GRAD_ROWS // 2, 2, HEAD_WIDTH)
    gathered = exchange(partial.reshape(split), ctx_axes)
    sums = call(sum_kernel, shape((rows, HEAD_WIDTH), BF16), 10**7, 3 * 10**5, "sum")(
        gathered.reshape(rows, HEAD_WIDTH)
    )
    result = exchange(sums.reshape(split), ctx_axes)
    grad_down, grad_up_query, grad_up_kv = call(
        functools.partial(finish_kernel, grad_scale),
        [
            shape((ranks, width), F32),
            shape((ADAPTER_RANK, width), F32),
            shape((2 * ADAPTER_RANK, HEAD_WIDTH), F32),
        ],
        10**6,
        5 * 10**5,
        "finish",
    )(result.reshape(rows, HEAD_WIDTH))
    return grad_query, key_gradient, value_gradient, grad_down, grad_up_query, grad_up_kv


def solution(mesh):
    ctx, peers = mesh.devices.shape
    by_ring = Mesh(
        mesh.devices.reshape(RINGS, ctx // RINGS, peers), ("ring", "place", "head")
    )
    both = P(("ring", "place"), "head")
    over_head = P(None, "head")
    return jax.shard_map(
        on_device,
        mesh=by_ring,
        in_specs=(both,) * 5 + (over_head,) * 3,
        out_specs=(both,) * 3 + (over_head,) * 3,
        check_vma=False,
    )
```

time: 199 us -> 110 us (0.55)
  waiting for transfers between devices: 100 us -> 6.37 us
  blocking collectives: 25.2 us -> 71 us
  matrix products: 22.5 us -> 0 us
  Pallas kernels: 0 us -> 15 us
  between operations: 14.3 us -> 0.73 us
  starting transfers between devices: 18.7 us -> 8.11 us
  local copies, waits for them, and re-layouts: 14.1 us -> 8.21 us
  other arithmetic: 3.74 us -> 0 us
    all_gather x1 -> x0, waiting for transfers between devices: 80.2 us -> none  [on_device(): gathered = lax.all_gather(stacked, 'ctx', axis=0, tiled=True)]
    all_to_all x1 -> x4, blocking collectives: 25.2 us -> 71 us  [exchange(): return lax.all_to_all(blocks, axis, split_axis=0, concat_axis=0, tiled=True)]
    dot_general x19 -> x0, matrix products: 22.5 us -> none  [the longest x1 4.39 us: on_device(): jnp.einsum('jgts,tjge->sje', score_qk, gradient_rows, preferred_element_t...]
    pallas_call x0 -> x8, Pallas kernels: none -> 15 us  [the longest x1 4.87 us: on_device(): call(local_kernel, [shape((tokens, width), BF16), shape(block, F32), shap...]
    all_to_all x3 -> x1, waiting for transfers between devices: 19.9 us -> 6.37 us  [exchange(): return lax.all_to_all(blocks, axis, split_axis=0, concat_axis=0, tiled=True)]
    all_to_all x3 -> x1, starting transfers between devices: 18.7 us -> 8.11 us  [exchange(): return lax.all_to_all(blocks, axis, split_axis=0, concat_axis=0, tiled=True)]
    another operation x1 -> x0, local copies, waits for them, and re-layouts: 4.06 us -> none
    broadcast_in_dim x3 -> x0, local copies, waits for them, and re-layouts: 2.44 us -> none  [copy_for_each(): copies = jnp.broadcast_to(array, (lax.axis_size(axis), *array.shape))]
  transfers between devices with their start and end apart: 4 -> 1, of which waited for: 3 -> 1; matrix products, arithmetic and copies ran while one was open for 7% -> 0% of each run, Pallas kernels for 0% -> 7%
where the time goes in v1:
time: 110 us; the launch traced here: 109 us
  blocking collectives  71 us (65%)
  Pallas kernels  15 us (14%)
  local copies, waits for them, and re-layouts  8.21 us (7%)
  starting transfers between devices  8.11 us (7%)
  waiting for transfers between devices  6.37 us (6%)
    all_to_all x4, blocking collectives, exchange(): return lax.all_to_all(blocks, axis, split_axis=0, concat_axis=0, tiled=True)  71 us
    unnamed x34, local copies, waits for them, and re-layouts  8.21 us
    all_to_all x1, starting transfers between devices, exchange(): return lax.all_to_all(blocks, axis, split_axis=0, concat_axis=0, tiled=True)  8.11 us
    all_to_all x1, waiting for transfers between devices, exchange(): return lax.all_to_all(blocks, axis, split_axis=0, concat_axis=0, tiled=True)  6.37 us
    pallas_call x1, Pallas kernels, on_device(): call(local_kernel, [shape((tokens, width), BF16), shape(block, F32), shap...  4.87 us
    pallas_call x1, Pallas kernels, on_device(): pl.pallas_call(states_kernel, in_specs=[hbm] * 4, out_shape=[shape((size,...  2.72 us
    pallas_call x1, Pallas kernels, on_device(): call(functools.partial(grads_kernel, att_scale), [shape((tokens, width),...  2.66 us
    pallas_call x1, Pallas kernels, on_device(): call(low_kernel, shape((ranks, tokens), BF16), 10 ** 8, 2 * 10 ** 6, 'low...  2.32 us
  transfers between devices with their start and end apart: 1, of which 1 were waited for; matrix products, arithmetic and copies ran while one was open for 0% of the time, Pallas kernels for 7%

profile of v1, /device:TPU:2, one launch (start us, length us, event | category | flops | bytes accessed | tf_op | source)
XLA Modules:
  0.0 109.4 jit_solution(13805802528242779555)
XLA Ops:
  0.6 2.7 %states.1 = (bf16[8,32,128]{2,1,0:T(8,128)(2,1)}, bf16[256,128]{1,0:T(8,128)(2,1)}) custom-call(bf16[512,1024]{1,0:T(8,128)(2,1)} %q_ref.3, bf16[512,1024]{1,0:T(8,128)(2,1)} %d_ref.5, bf16[512,128]{1,0:T(8,128)(2,1)} %k_ref.3, bf16[512,128]{1,0:T(8,128)(2,1)} %v_ref.3), custom_call_target="tpu_custom_call" | custom-call | flops 100000000 | bytes 2000000 | tf_op jit(solution)/shard_map/states/pallas_call | solution.py:281
  3.4 18.7 %all_to_all.25.x_ref = bf16[8,32,128]{2,1,0:T(8,128)(2,1)S(1)} all-to-all(bf16[8,32,128]{2,1,0:T(8,128)(2,1)} %get-tuple-element.21), channel_id=1, replica_groups=mesh['ring'=8,'place'=8,'head'=8] {'place'}, dimensions={0} | all-to-all | bytes 131072 | tf_op jit(solution)/shard_map/all_to_all | solution.py:266
  22.1 0.9 scan.1
  22.9 0.0 copy-start.15
  23.0 0.6 copy-done.15
  23.5 8.1 %all-to-all-start.1 = ((bf16[64,32,128]{2,1,0:T(8,128)(2,1)}), bf16[64,32,128]{2,1,0:T(8,128)(2,1)S(1)}, u32[]{:S(2)}, u32[]{:S(2)}) async-start(bf16[64,32,128]{2,1,0:T(8,128)(2,1)} %get-tuple-element.22), calls=%async_computation.1 | async-start | bytes 1048576 | tf_op jit(solution)/shard_map/all_to_all | solution.py:266
  31.7 0.0 copy-start.8
  31.7 0.0 copy-start.12
  31.7 2.3 %low.1.low_ref = bf16[48,512]{1,0:T(8,128)(2,1)} custom-call(bf16[512,1024]{1,0:T(8,128)(2,1)} %hidden_ref.3, bf16[48,1024]{1,0:T(8,128)(2,1)} %down_ref.1, bf16[256,128]{1,0:T(8,128)(2,1)} %get-tuple-element.23.chunk_ref.after_ref), custom_call_target="tpu_custom_call" | custom-call | flops 100000000 | bytes 2000000 | tf_op jit(solution)/shard_map/low/pallas_call | solution.py:304
  34.0 0.0 copy-done.8
  34.0 0.0 copy-done.12
  34.0 0.0 copy-start.1
  34.0 1.2 %copy-done.1 = bf16[512,1024]{1,0:T(8,128)(2,1)S(1)} copy-done((bf16[512,1024]{1,0:T(8,128)(2,1)S(1)}, bf16[512,1024]{1,0:T(8,128)(2,1)}, u32[]{:S(2)}) %copy-start.1) | copy-done | bytes 1048600
  35.2 0.0 copy-start.4
  35.2 1.2 %copy-done.4 = bf16[512,1024]{1,0:T(8,128)(2,1)S(1)} copy-done((bf16[512,1024]{1,0:T(8,128)(2,1)S(1)}, bf16[512,1024]{1,0:T(8,128)(2,1)}, u32[]{:S(2)}) %copy-start.4) | copy-done | bytes 1048600
  36.5 0.0 copy-start.9
  36.5 0.9 copy-done.9
  37.4 0.0 copy-start.16
  37.4 0.7 copy-done.16
  38.0 0.0 copy-start.2
  38.1 0.0 copy-start.7
  38.1 0.0 copy-start.13
  38.1 4.9 %local.1 = (bf16[512,1024]{1,0:T(8,128)(2,1)S(1)}, f32[512,128]{1,0:T(8,128)S(1)}, f32[512,128]{1,0:T(8,128)S(1)}, bf16[512,256]{1,0:T(8,128)(2,1)S(1)}) custom-call(bf16[512,1024]{1,0:T(8,128)(2,1)S(1)} %copy-done.4, bf16[512,1024]{1,0:T(8,128)(2,1)S(1)} %copy-done.1, bf16[512,128]{1,0:T(8,128)(2,1)S(1)} %copy-done.8, bf16[512,128]{1,0:T(8,128)(2,1)S(1)} %copy-done.9, ...), custom_call_target="tpu_custom_call" | custom-call | flops 2000000000 | bytes 5000000 | tf_op jit(solution)/shard_map/local/pallas_call | solution.py:322
  42.9 0.0 copy-start.5
  42.9 0.7 copy-done.5
  43.6 6.4 %all-to-all-done.1.state_ref = bf16[64,32,128]{2,1,0:T(8,128)(2,1)S(1)} async-done(((bf16[64,32,128]{2,1,0:T(8,128)(2,1)}), bf16[64,32,128]{2,1,0:T(8,128)(2,1)S(1)}, u32[]{:S(2)}, u32[]{:S(2)}) %all-to-all-start.1) | async-done | bytes 524320 | tf_op jit(solution)/shard_map/all_to_all | solution.py:266
  50.0 0.0 copy-done.2
  50.0 0.0 copy-done.7
  50.0 0.0 copy-done.13
  50.0 0.0 copy-start.6
  50.0 0.9 copy-done.6
  51.0 0.0 copy-start.14
  51.0 0.7 copy-done.14
  51.7 2.7 %grads.1 = (bf16[512,1024]{1,0:T(8,128)(2,1)}, bf16[512,128]{1,0:T(8,128)(2,1)}, bf16[512,128]{1,0:T(8,128)(2,1)}, bf16[8,96,512]{2,1,0:T(8,128)(2,1)S(1)}) custom-call(bf16[64,32,128]{2,1,0:T(8,128)(2,1)S(1)} %all-to-all-done.1.state_ref, bf16[512,1024]{1,0:T(8,128)(2,1)S(1)} %get-tuple-element.25.gq_ref, f32[512,128]{1,0:T(8,128)S(1)} %get-tuple-element.26.kgl_ref, ...), custom_call_target="tpu_custom_call" | custom-call | flops 200000000 | bytes 5000000 | tf_op jit(solution)/shard_map/grads/pallas_call | solution.py:335
  54.3 0.0 copy-start
  54.3 0.0 copy-start.10
  54.3 0.0 copy-start.11
  54.3 16.6 %all_to_all.26.parts_ref = bf16[8,96,512]{2,1,0:T(8,128)(2,1)S(1)} all-to-all(bf16[8,96,512]{2,1,0:T(8,128)(2,1)S(1)} %get-tuple-element.32), channel_id=1, replica_groups=mesh['ring'=8,'place'=8,'head'=8] {'head'}, dimensions={0} | all-to-all | bytes 1572864 | tf_op jit(solution)/shard_map/all_to_all | solution.py:266
  70.9 0.0 copy-done
  70.9 0.0 copy-done.10
  70.9 0.0 copy-done.11
  70.9 0.0 copy-start.3
  70.9 1.2 %copy-done.3 = bf16[512,1024]{1,0:T(8,128)(2,1)S(1)} copy-done((bf16[512,1024]{1,0:T(8,128)(2,1)S(1)}, bf16[512,1024]{1,0:T(8,128)(2,1)}, u32[]{:S(2)}) %copy-start.3) | copy-done | bytes 1048600
  72.1 0.5 down.1
  72.6 19.0 %all_to_all.27 = bf16[64,5,2,128]{3,2,1,0:T(2,128)(2,1)S(1)} all-to-all(bf16[64,5,2,128]{3,2,1,0:T(2,128)(2,1)S(1)} %bitcast.4), channel_id=1, replica_groups=mesh['ring'=8,'place'=8,'head'=8] {'ring','place'}, dimensions={0} | all-to-all | bytes 327680 | tf_op jit(solution)/shard_map/all_to_all | solution.py:266
  91.6 0.3 sum.1
  91.9 16.8 %all_to_all.28 = bf16[64,5,2,128]{3,2,1,0:T(2,128)(2,1)S(1)} all-to-all(bf16[64,5,2,128]{3,2,1,0:T(2,128)(2,1)S(1)} %bitcast.7), channel_id=1, replica_groups=mesh['ring'=8,'place'=8,'head'=8] {'ring','place'}, dimensions={0} | all-to-all | bytes 327680 | tf_op jit(solution)/shard_map/all_to_all | solution.py:266
  108.7 0.7 finish.1
Async XLA Ops:
  22.9 0.6 copy-start.15
  23.5 26.5 %all-to-all-start.1 = ((bf16[64,32,128]{2,1,0:T(8,128)(2,1)}), bf16[64,32,128]{2,1,0:T(8,128)(2,1)S(1)}, u32[]{:S(2)}, u32[]{:S(2)}) async-start(bf16[64,32,128]{2,1,0:T(8,128)(2,1)} %get-tuple-element.22), calls=%async_computation.1 | async-start | bytes 1048576 | tf_op jit(solution)/shard_map/all_to_all | solution.py:266
  31.7 2.3 %copy-start.8 = (bf16[512,128]{1,0:T(8,128)(2,1)S(1)}, bf16[512,128]{1,0:T(8,128)(2,1)}, u32[]{:S(2)}) copy-start(bf16[512,128]{1,0:T(8,128)(2,1)} %k_ref.3) | copy-start | bytes 393220
  31.7 2.3 %copy-start.12 = (bf16[256,128]{1,0:T(8,128)(2,1)S(1)}, bf16[256,128]{1,0:T(8,128)(2,1)}, u32[]{:S(2)}) copy-start(bf16[256,128]{1,0:T(8,128)(2,1)} %get-tuple-element.23.chunk_ref.after_ref) | copy-start | bytes 196612
  34.0 1.2 %copy-start.1 = (bf16[512,1024]{1,0:T(8,128)(2,1)S(1)}, bf16[512,1024]{1,0:T(8,128)(2,1)}, u32[]{:S(2)}) copy-start(bf16[512,1024]{1,0:T(8,128)(2,1)} %d_ref.5) | copy-start | bytes 3145732
  35.2 1.2 %copy-start.4 = (bf16[512,1024]{1,0:T(8,128)(2,1)S(1)}, bf16[512,1024]{1,0:T(8,128)(2,1)}, u32[]{:S(2)}) copy-start(bf16[512,1024]{1,0:T(8,128)(2,1)} %q_ref.3) | copy-start | bytes 3145732
  36.5 0.9 copy-start.9
  37.4 0.7 copy-start.16
  38.0 12.0 %copy-start.2 = (bf16[512,1024]{1,0:T(8,128)(2,1)S(1)}, bf16[512,1024]{1,0:T(8,128)(2,1)}, u32[]{:S(2)}) copy-start(bf16[512,1024]{1,0:T(8,128)(2,1)} %d_ref.5) | copy-start | bytes 3145732
  38.1 12.0 %copy-start.7 = (bf16[48,512]{1,0:T(8,128)(2,1)S(1)}, bf16[48,512]{1,0:T(8,128)(2,1)}, u32[]{:S(2)}) copy-start(bf16[48,512]{1,0:T(8,128)(2,1)} %low.1.low_ref) | copy-start | bytes 147460
  38.1 12.0 %copy-start.13 = (bf16[16,1024]{1,0:T(8,128)(2,1)S(1)}, bf16[16,1024]{1,0:T(8,128)(2,1)}, u32[]{:S(2)}) copy-start(bf16[16,1024]{1,0:T(8,128)(2,1)} %up_ref.1) | copy-start | bytes 98308
  42.9 0.7 copy-start.5
  50.0 1.0 copy-start.6
  51.0 0.7 copy-start.14
  54.3 16.6 %copy-start = (bf16[512,1024]{1,0:T(8,128)(2,1)S(1)}, bf16[512,1024]{1,0:T(8,128)(2,1)}, u32[]{:S(2)}) copy-start(bf16[512,1024]{1,0:T(8,128)(2,1)} %hidden_ref.3) | copy-start | bytes 3145732
  54.3 16.6 %copy-start.10 = (bf16[512,128]{1,0:T(8,128)(2,1)S(1)}, bf16[512,128]{1,0:T(8,128)(2,1)}, u32[]{:S(2)}) copy-start(bf16[512,128]{1,0:T(8,128)(2,1)} %get-tuple-element.16.key_ref) | copy-start | bytes 393220
  54.3 16.6 %copy-start.11 = (bf16[512,128]{1,0:T(8,128)(2,1)S(1)}, bf16[512,128]{1,0:T(8,128)(2,1)}, u32[]{:S(2)}) copy-start(bf16[512,128]{1,0:T(8,128)(2,1)} %get-tuple-element.17.value_ref) | copy-start | bytes 393220
  70.9 1.2 %copy-start.3 = (bf16[512,1024]{1,0:T(8,128)(2,1)S(1)}, bf16[512,1024]{1,0:T(8,128)(2,1)}, u32[]{:S(2)}) copy-start(bf16[512,1024]{1,0:T(8,128)(2,1)} %get-tuple-element.15.query_ref) | copy-start | bytes 3145732

commit v2 on v1

--- a/solution.py
+++ b/solution.py
@@ -91,33 +91,35 @@
     chunk_ref[pl.ds(HEAD_WIDTH, HEAD_WIDTH), :] = state_qo[1].astype(BF16)
 
 
-def scan_kernel(x_ref, out_ref, token_ref):
+def ring_kernel(x_ref, chunk_ref, after_ref, out_ref, chunk_out_ref):
     size, rows, _ = x_ref.shape
     rows //= 2
     ring = lax.axis_index("ring")
-    kv = [x_ref[i, pl.ds(0, rows), :].astype(F32) for i in range(size)]
-    qo = [x_ref[i, pl.ds(rows, rows), :].astype(F32) for i in range(size)]
-    nothing = jnp.zeros_like(kv[0])
-    before, after = [nothing], [nothing]
+    total = sum(x_ref[i].astype(F32) for i in range(size))
+    for there in range(out_ref.shape[0]):
+        out_ref[there] = jnp.where(ring < there, total[:rows], total[rows:]).astype(BF16)
+    chunk_out_ref[...] = chunk_ref[...]
+
+
+def scan_kernel(x_ref, rings_ref, after_ref, out_ref):
+    size, rows, _ = x_ref.shape
+    rows //= 2
+    ring = lax.axis_index("ring")
+    before = jnp.zeros((rows, HEAD_WIDTH), F32)
+    after = jnp.zeros((rows, HEAD_WIDTH), F32)
+    for there in range(rings_ref.shape[0]):
+        part = rings_ref[there].astype(F32)
+        before += jnp.where(there < ring, part, 0.0)
+        after += jnp.where(there > ring, part, 0.0)
     for i in range(size):
-        before.append(before[-1] + kv[i])
-        after.append(after[-1] + qo[size - 1 - i])
-    for there in range(out_ref.shape[0] // size):
-        for i in range(size):
-            kv_part = jnp.where(
-                ring < there, before[size], jnp.where(ring == there, before[i], nothing)
-            )
-            qo_part = jnp.where(
-                ring > there, after[size], jnp.where(ring == there, after[size - 1 - i], nothing)
-            )
-            out_ref[there * size + i, pl.ds(0, rows), :] = kv_part.astype(BF16)
-            out_ref[there * size + i, pl.ds(rows, rows), :] = qo_part.astype(BF16)
-    token_ref[...] = jnp.zeros_like(token_ref)
-
-
-def local_kernel(
-    q_ref, d_ref, k_ref, v_ref, chunk_ref, after_ref, gq_ref, kg_ref, vg_ref, kv_ref
-):
+        last = size - 1 - i
+        out_ref[i, pl.ds(0, rows), :] = before.astype(BF16)
+        out_ref[last, pl.ds(rows, rows), :] = after.astype(BF16)
+        before += x_ref[i, pl.ds(0, rows), :].astype(F32)
+        after += x_ref[last, pl.ds(rows, rows), :].astype(F32)
+
+
+def local_kernel(q_ref, d_ref, k_ref, v_ref, chunk_ref, gq_ref, near_ref):
     tokens, width = q_ref.shape
     half = tokens // 2
     row, column = grid2(half, half)
@@ -126,8 +128,6 @@
     def masked(scores):
         return jnp.where(causal, scores, 0.0).astype(BF16)
 
-    kv_ref[:, pl.ds(0, HEAD_WIDTH)] = k_ref[...]
-    kv_ref[:, pl.ds(HEAD_WIDTH, HEAD_WIDTH)] = v_ref[...]
     state_kv = chunk_ref[pl.ds(0, HEAD_WIDTH), :]
     state_qo = chunk_ref[pl.ds(HEAD_WIDTH, HEAD_WIDTH), :]
     for i in range(2):
@@ -148,8 +148,9 @@
             gq_ref[rows, at] = grad_query.astype(BF16)
             key_gradient += tn(score_do, q)
             value_gradient += tn(score_qk, d)
-        kg_ref[rows, :] = key_gradient
-        vg_ref[rows, :] = value_gradient
+        both = (key_gradient.astype(BF16), value_gradient.astype(BF16))
+        for j, columns in enumerate((*both, k, v)):
+            near_ref[rows, pl.ds(j * HEAD_WIDTH, HEAD_WIDTH)] = columns
 
 
 def low_kernel(hidden_ref, down_ref, after_ref, out_ref):
@@ -157,40 +158,48 @@
 
 
 def grads_kernel(
-    scale, state_ref, gq_ref, kgl_ref, vgl_ref, d_ref, kv_ref, up_ref, kvup_ref, low_ref,
+    scale, state_ref, gq_ref, near_ref, d_ref, up_ref, kvup_ref, low_ref,
     query_ref, key_ref, value_ref, send_ref,
 ):
     tokens, width = d_ref.shape
+    half = tokens // 2
     rank = low_ref.shape[0]
-    size = state_ref.shape[0] // RINGS
-    state_rows = state_ref.shape[1] // 2
-    prefix, suffix = [], []
-    for i in range(size):
-        total = sum(state_ref[ring * size + i].astype(F32) for ring in range(RINGS))
-        prefix.append(total[:state_rows])
-        suffix.append(total[state_rows:])
-    prefix = jnp.concatenate(prefix, axis=0).astype(BF16)
-    suffix = jnp.concatenate(suffix, axis=0).astype(BF16)
-    k, v = kv_ref[:, pl.ds(0, HEAD_WIDTH)], kv_ref[:, pl.ds(HEAD_WIDTH, HEAD_WIDTH)]
-    key_gradient = (scale * (kgl_ref[...] + nt(v, suffix))).astype(BF16)
-    value_gradient = (scale * (vgl_ref[...] + nn(k, suffix))).astype(BF16)
-    key_ref[...] = key_gradient
-    value_ref[...] = value_gradient
-    back = jnp.zeros((ADAPTER_RANK, tokens), F32)
-    for h in range(width // HEAD_WIDTH):
-        at = pl.ds(h * HEAD_WIDTH, HEAD_WIDTH)
-        grad_query = gq_ref[:, at].astype(F32) + nt(d_ref[:, at], prefix)
-        grad_query = (scale * grad_query).astype(BF16)
-        query_ref[:, at] = grad_query
-        back += nt(up_ref[:, at], grad_query)
-    whole = jnp.concatenate(
-        [
-            back,
-            nt(kvup_ref[pl.ds(0, ADAPTER_RANK), :], key_gradient),
-            nt(kvup_ref[pl.ds(ADAPTER_RANK, ADAPTER_RANK), :], value_gradient),
-        ],
-        axis=0,
-    ).astype(BF16)
+    size, state_rows, _ = state_ref.shape
+    state_rows //= 2
+    prefix, suffix = (
+        jnp.concatenate(
+            [state_ref[i, pl.ds(j * state_rows, state_rows), :] for i in range(size)], axis=0
+        )
+        for j in range(2)
+    )
+    backs = []
+    for i in range(2):
+        rows = pl.ds(i * half, half)
+        local_k, local_v, k, v = (
+            near_ref[rows, pl.ds(j * HEAD_WIDTH, HEAD_WIDTH)] for j in range(4)
+        )
+        key_gradient = (scale * (local_k.astype(F32) + nt(v, suffix))).astype(BF16)
+        value_gradient = (scale * (local_v.astype(F32) + nn(k, suffix))).astype(BF16)
+        key_ref[rows, :] = key_gradient
+        value_ref[rows, :] = value_gradient
+        back = jnp.zeros((ADAPTER_RANK, half), F32)
+        for h in range(width // HEAD_WIDTH):
+            at = pl.ds(h * HEAD_WIDTH, HEAD_WIDTH)
+            grad_query = gq_ref[rows, at].astype(F32) + nt(d_ref[rows, at], prefix)
+            grad_query = (scale * grad_query).astype(BF16)
+            query_ref[rows, at] = grad_query
+            back += nt(up_ref[:, at], grad_query)
+        backs.append(
+            jnp.concatenate(
+                [
+                    back,
+                    nt(kvup_ref[pl.ds(0, ADAPTER_RANK), :], key_gradient),
+                    nt(kvup_ref[pl.ds(ADAPTER_RANK, ADAPTER_RANK), :], value_gradient),
+                ],
+                axis=0,
+            )
+        )
+    whole = jnp.concatenate(backs, axis=1).astype(BF16)
     for i in range(send_ref.shape[0]):
         send_ref[i, pl.ds(0, rank), :] = whole
         send_ref[i, pl.ds(rank, rank), :] = low_ref[...]
@@ -300,37 +309,33 @@
     )(query, d_out, key, value)
     ring_states = exchange(sent, "place")
 
-    vmem, anywhere = (pl.BlockSpec(memory_space=space) for space in (pltpu.VMEM, pl.ANY))
-    low = call(
-        low_kernel,
-        shape((ranks, tokens), BF16),
-        10**8,
-        2 * 10**6,
-        "low",
-        ALONE,
-        in_specs=[vmem, vmem, anywhere],
-    )(hidden, down, chunk)
-
-    scanned, token = call(
-        scan_kernel,
-        [shape((ctx, state_rows, HEAD_WIDTH), BF16), shape((8, HEAD_WIDTH), F32)],
+    low = call(low_kernel, shape((ranks, tokens), BF16), 10**8, 2 * 10**6, "low")(
+        hidden, down, chunk
+    )
+
+    ring_sums, chunk = call(
+        ring_kernel,
+        [shape((RINGS, state_rows // 2, HEAD_WIDTH), BF16), shape((2 * HEAD_WIDTH, HEAD_WIDTH), BF16)],
         10**6,
-        6 * 10**5,
-        "scan",
-    )(ring_states)
-    around = exchange(scanned, ctx_axes)
-    local_q, local_k, local_v, key_value = call(
+        2 * 10**5,
+        "ring",
+    )(ring_states, chunk, low)
+    other_rings = exchange(ring_sums, "ring")
+    local_q, near = call(
         local_kernel,
-        [
-            shape((tokens, width), BF16),
-            shape(block, F32),
-            shape(block, F32),
-            shape((tokens, 2 * HEAD_WIDTH), BF16),
-        ],
+        [shape((tokens, width), BF16), shape((tokens, 4 * HEAD_WIDTH), BF16)],
         2 * 10**9,
         5 * 10**6,
         "local",
-    )(query, d_out, key, value, chunk, token)
+    )(query, d_out, key, value, chunk)
+    scanned = call(
+        scan_kernel,
+        shape((size, state_rows, HEAD_WIDTH), BF16),
+        10**6,
+        2 * 10**5,
+        "scan",
+    )(ring_states, other_rings, near)
+    around = exchange(scanned, "place")
 
     grad_query, key_gradient, value_gradient, copies = call(
         functools.partial(grads_kernel, att_scale),
@@ -344,7 +349,7 @@
         5 * 10**6,
         "grads",
     )(
-        around, local_q, local_k, local_v, d_out, key_value, up_query, kv_up, low
+        around, local_q, near, d_out, up_query, kv_up, low
     )
     both_parts = exchange(copies, "head")
     rows = ctx * GRAD_ROWS

time: 110 us -> 106 us (0.964)
  starting transfers between devices: 8.11 us -> 17.6 us
  blocking collectives: 71 us -> 63.1 us
  local copies, waits for them, and re-layouts: 8.21 us -> 3.71 us
  Pallas kernels: 15 us -> 12.1 us
  waiting for transfers between devices: 6.37 us -> 8.61 us
    all_to_all x1 -> x2, starting transfers between devices: 8.11 us -> 17.6 us  [exchange(): return lax.all_to_all(blocks, axis, split_axis=0, concat_axis=0, tiled=True)]
    all_to_all x4, blocking collectives: 71 us -> 63.1 us  [exchange(): return lax.all_to_all(blocks, axis, split_axis=0, concat_axis=0, tiled=True)]
    unnamed x34 -> x26, local copies, waits for them, and re-layouts: 8.21 us -> 3.71 us
    all_to_all x1 -> x2, waiting for transfers between devices: 6.37 us -> 8.61 us  [exchange(): return lax.all_to_all(blocks, axis, split_axis=0, concat_axis=0, tiled=True)]
    pallas_call x3 -> x4, Pallas kernels: 8.08 us -> 5.93 us  [the longest x1 4.85 us: on_device(): call(local_kernel, [shape((tokens, width), BF16), shape((tokens, 4 * HEAD...]
  transfers between devices with their start and end apart: 1 -> 2, of which waited for: 1 -> 2; matrix products, arithmetic and copies ran while one was open for 0% -> 0% of each run, Pallas kernels for 7% -> 5%
where the time goes in v2:
time: 106 us
  blocking collectives  63.1 us (60%)
  starting transfers between devices  17.6 us (17%)
  Pallas kernels  12.1 us (11%)
  waiting for transfers between devices  8.61 us (8%)
  local copies, waits for them, and re-layouts  3.71 us (4%)
    all_to_all x4, blocking collectives, exchange(): return lax.all_to_all(blocks, axis, split_axis=0, concat_axis=0, tiled=True)  63.1 us
    all_to_all x2, starting transfers between devices, exchange(): return lax.all_to_all(blocks, axis, split_axis=0, concat_axis=0, tiled=True)  17.6 us
    all_to_all x2, waiting for transfers between devices, exchange(): return lax.all_to_all(blocks, axis, split_axis=0, concat_axis=0, tiled=True)  8.61 us
    pallas_call x1, Pallas kernels, on_device(): call(local_kernel, [shape((tokens, width), BF16), shape((tokens, 4 * HEAD...  4.85 us
    unnamed x26, local copies, waits for them, and re-layouts  3.71 us
    pallas_call x1, Pallas kernels, on_device(): pl.pallas_call(states_kernel, in_specs=[hbm] * 4, out_shape=[shape((size,...  2.74 us
  transfers between devices with their start and end apart: 2, of which 2 were waited for; matrix products, arithmetic and copies ran while one was open for 0% of the time, Pallas kernels for 5%

profile of v2, /device:TPU:2, one launch (start us, length us, event | category | flops | bytes accessed | tf_op | source)
XLA Modules:
  0.0 105.8 jit_solution(4547105009784260104)
XLA Ops:
  0.6 0.0 copy-start.10
  0.6 2.7 %states.1 = (bf16[8,32,128]{2,1,0:T(8,128)(2,1)}, bf16[256,128]{1,0:T(8,128)(2,1)}) custom-call(bf16[512,1024]{1,0:T(8,128)(2,1)} %q_ref.3, bf16[512,1024]{1,0:T(8,128)(2,1)} %d_ref.5, bf16[512,128]{1,0:T(8,128)(2,1)} %k_ref.3, bf16[512,128]{1,0:T(8,128)(2,1)} %v_ref.3), custom_call_target="tpu_custom_call" | custom-call | flops 100000000 | bytes 2000000 | tf_op jit(solution)/shard_map/states/pallas_call | solution.py:290
  3.4 0.0 copy-start.5
  3.4 10.5 %all-to-all-start = ((bf16[8,32,128]{2,1,0:T(8,128)(2,1)}), bf16[8,32,128]{2,1,0:T(8,128)(2,1)S(1)}, u32[]{:S(2)}, u32[]{:S(2)}) async-start(bf16[8,32,128]{2,1,0:T(8,128)(2,1)} %get-tuple-element.19), calls=%async_computation | async-start | bytes 131072 | tf_op jit(solution)/shard_map/all_to_all | solution.py:275
  13.9 0.0 copy-done.10
  13.9 0.0 copy-done.5
  13.9 0.0 copy-start
  13.9 1.2 %copy-done = bf16[512,1024]{1,0:T(8,128)(2,1)S(1)} copy-done((bf16[512,1024]{1,0:T(8,128)(2,1)S(1)}, bf16[512,1024]{1,0:T(8,128)(2,1)}, u32[]{:S(2)}) %copy-start) | copy-done | bytes 1048600
  15.1 0.0 copy-start.2
  15.1 0.0 copy-start.7
  15.1 0.4 low.1.after_ref.low_ref
  15.5 0.0 copy-start.6
  15.6 6.7 %all-to-all-done.x_ref = bf16[8,32,128]{2,1,0:T(8,128)(2,1)S(1)} async-done(((bf16[8,32,128]{2,1,0:T(8,128)(2,1)}), bf16[8,32,128]{2,1,0:T(8,128)(2,1)S(1)}, u32[]{:S(2)}, u32[]{:S(2)}) %all-to-all-start) | async-done | bytes 65568 | tf_op jit(solution)/shard_map/all_to_all | solution.py:275
  22.2 0.6 ring.1
  22.9 7.1 %all-to-all-start.1 = ((bf16[8,16,128]{2,1,0:T(8,128)(2,1)}), bf16[8,16,128]{2,1,0:T(8,128)(2,1)S(1)}, u32[]{:S(2)}, u32[]{:S(2)}) async-start(bf16[8,16,128]{2,1,0:T(8,128)(2,1)} %get-tuple-element.21), calls=%async_computation.1 | async-start | bytes 65536 | tf_op jit(solution)/shard_map/all_to_all | solution.py:275
  30.0 0.0 copy-done.2
  30.0 0.0 copy-done.7
  30.0 0.0 copy-done.6
  30.0 0.0 copy-start.4
  30.0 1.2 %copy-done.4 = bf16[512,1024]{1,0:T(8,128)(2,1)S(1)} copy-done((bf16[512,1024]{1,0:T(8,128)(2,1)S(1)}, bf16[512,1024]{1,0:T(8,128)(2,1)}, u32[]{:S(2)}) %copy-start.4) | copy-done | bytes 1048600
  31.2 4.8 %local.1 = (bf16[512,1024]{1,0:T(8,128)(2,1)S(1)}, bf16[512,512]{1,0:T(8,128)(2,1)S(1)}) custom-call(bf16[512,1024]{1,0:T(8,128)(2,1)S(1)} %copy-done.4, bf16[512,1024]{1,0:T(8,128)(2,1)S(1)} %copy-done.2, bf16[512,128]{1,0:T(8,128)(2,1)S(1)} %copy-done.6, bf16[512,128]{1,0:T(8,128)(2,1)S(1)} %copy-done.7, bf16[256,128]{1,0:T(8,128)(2,1)S(1)} %get-tuple-element.22.chunk_ref), custom_call_target="tpu_custom_call" | custom-call | flops 2000000000 | bytes 5000000 | tf_op jit(solution)/shard_map/local/pallas_call | solution.py:324
  36.1 1.9 %all-to-all-done.1.rings_ref = bf16[8,16,128]{2,1,0:T(8,128)(2,1)S(1)} async-done(((bf16[8,16,128]{2,1,0:T(8,128)(2,1)}), bf16[8,16,128]{2,1,0:T(8,128)(2,1)S(1)}, u32[]{:S(2)}, u32[]{:S(2)}) %all-to-all-start.1) | async-done | bytes 32800 | tf_op jit(solution)/shard_map/all_to_all | solution.py:275
  38.0 0.0 copy-start.11
  38.0 0.0 copy-start.12
  38.1 10.8 %all_to_all.30.state_ref = bf16[8,32,128]{2,1,0:T(8,128)(2,1)S(1)} all-to-all(bf16[8,32,128]{2,1,0:T(8,128)(2,1)S(1)} %scan.1), channel_id=1, replica_groups=mesh['ring'=8,'place'=8,'head'=8] {'place'}, dimensions={0} | all-to-all | bytes 131072 | tf_op jit(solution)/shard_map/all_to_all | solution.py:275
  48.8 0.0 copy-done.11
  48.8 0.0 copy-done.12
  48.8 1.9 %grads.1 = (bf16[512,1024]{1,0:T(8,128)(2,1)}, bf16[512,128]{1,0:T(8,128)(2,1)}, bf16[512,128]{1,0:T(8,128)(2,1)}, bf16[8,96,512]{2,1,0:T(8,128)(2,1)S(1)}) custom-call(bf16[8,32,128]{2,1,0:T(8,128)(2,1)S(1)} %all_to_all.30.state_ref, bf16[512,1024]{1,0:T(8,128)(2,1)S(1)} %get-tuple-element.24.gq_ref, ...), custom_call_target="tpu_custom_call" | custom-call | flops 200000000 | bytes 5000000 | tf_op jit(solution)/shard_map/grads/pallas_call | solution.py:340
  50.7 0.0 copy-start.1
  50.7 0.0 copy-start.8
  50.7 0.0 copy-start.9
  50.7 16.5 %all_to_all.31.parts_ref = bf16[8,96,512]{2,1,0:T(8,128)(2,1)S(1)} all-to-all(bf16[8,96,512]{2,1,0:T(8,128)(2,1)S(1)} %get-tuple-element.28), channel_id=1, replica_groups=mesh['ring'=8,'place'=8,'head'=8] {'head'}, dimensions={0} | all-to-all | bytes 1572864 | tf_op jit(solution)/shard_map/all_to_all | solution.py:275
  67.3 0.0 copy-done.1
  67.3 0.0 copy-done.8
  67.3 0.0 copy-done.9
  67.3 0.0 copy-start.3
  67.3 1.2 %copy-done.3 = bf16[512,1024]{1,0:T(8,128)(2,1)S(1)} copy-done((bf16[512,1024]{1,0:T(8,128)(2,1)S(1)}, bf16[512,1024]{1,0:T(8,128)(2,1)}, u32[]{:S(2)}) %copy-start.3) | copy-done | bytes 1048600
  68.5 0.5 down.1
  69.0 19.0 %all_to_all.32 = bf16[64,5,2,128]{3,2,1,0:T(2,128)(2,1)S(1)} all-to-all(bf16[64,5,2,128]{3,2,1,0:T(2,128)(2,1)S(1)} %bitcast.4), channel_id=1, replica_groups=mesh['ring'=8,'place'=8,'head'=8] {'ring','place'}, dimensions={0} | all-to-all | bytes 327680 | tf_op jit(solution)/shard_map/all_to_all | solution.py:275
  87.9 0.3 sum.1
  88.3 16.8 %all_to_all.33 = bf16[64,5,2,128]{3,2,1,0:T(2,128)(2,1)S(1)} all-to-all(bf16[64,5,2,128]{3,2,1,0:T(2,128)(2,1)S(1)} %bitcast.7), channel_id=1, replica_groups=mesh['ring'=8,'place'=8,'head'=8] {'ring','place'}, dimensions={0} | all-to-all | bytes 327680 | tf_op jit(solution)/shard_map/all_to_all | solution.py:275
  105.1 0.7 finish.1
  (1 shorter events, 0.0 us)
Async XLA Ops:
  0.6 13.2 %copy-start.10 = (bf16[48,1024]{1,0:T(8,128)(2,1)S(1)}, bf16[48,1024]{1,0:T(8,128)(2,1)}, u32[]{:S(2)}) copy-start(bf16[48,1024]{1,0:T(8,128)(2,1)} %down_ref.1) | copy-start | bytes 294916
  3.4 10.5 %copy-start.5 = (bf16[256,128]{1,0:T(8,128)(2,1)S(1)}, bf16[256,128]{1,0:T(8,128)(2,1)}, u32[]{:S(2)}) copy-start(bf16[256,128]{1,0:T(8,128)(2,1)} %get-tuple-element.20.after_ref.chunk_ref) | copy-start | bytes 196612
  3.4 18.8 %all-to-all-start = ((bf16[8,32,128]{2,1,0:T(8,128)(2,1)}), bf16[8,32,128]{2,1,0:T(8,128)(2,1)S(1)}, u32[]{:S(2)}, u32[]{:S(2)}) async-start(bf16[8,32,128]{2,1,0:T(8,128)(2,1)} %get-tuple-element.19), calls=%async_computation | async-start | bytes 131072 | tf_op jit(solution)/shard_map/all_to_all | solution.py:275
  13.9 1.2 %copy-start = (bf16[512,1024]{1,0:T(8,128)(2,1)S(1)}, bf16[512,1024]{1,0:T(8,128)(2,1)}, u32[]{:S(2)}) copy-start(bf16[512,1024]{1,0:T(8,128)(2,1)} %hidden_ref.3) | copy-start | bytes 3145732
  15.1 14.9 %copy-start.2 = (bf16[512,1024]{1,0:T(8,128)(2,1)S(1)}, bf16[512,1024]{1,0:T(8,128)(2,1)}, u32[]{:S(2)}) copy-start(bf16[512,1024]{1,0:T(8,128)(2,1)} %d_ref.5) | copy-start | bytes 3145732
  15.1 14.9 %copy-start.7 = (bf16[512,128]{1,0:T(8,128)(2,1)S(1)}, bf16[512,128]{1,0:T(8,128)(2,1)}, u32[]{:S(2)}) copy-start(bf16[512,128]{1,0:T(8,128)(2,1)} %v_ref.3) | copy-start | bytes 393220
  15.5 14.5 %copy-start.6 = (bf16[512,128]{1,0:T(8,128)(2,1)S(1)}, bf16[512,128]{1,0:T(8,128)(2,1)}, u32[]{:S(2)}) copy-start(bf16[512,128]{1,0:T(8,128)(2,1)} %k_ref.3) | copy-start | bytes 393220
  22.9 15.1 %all-to-all-start.1 = ((bf16[8,16,128]{2,1,0:T(8,128)(2,1)}), bf16[8,16,128]{2,1,0:T(8,128)(2,1)S(1)}, u32[]{:S(2)}, u32[]{:S(2)}) async-start(bf16[8,16,128]{2,1,0:T(8,128)(2,1)} %get-tuple-element.21), calls=%async_computation.1 | async-start | bytes 65536 | tf_op jit(solution)/shard_map/all_to_all | solution.py:275
  30.0 1.2 %copy-start.4 = (bf16[512,1024]{1,0:T(8,128)(2,1)S(1)}, bf16[512,1024]{1,0:T(8,128)(2,1)}, u32[]{:S(2)}) copy-start(bf16[512,1024]{1,0:T(8,128)(2,1)} %q_ref.3) | copy-start | bytes 3145732
  38.0 10.8 %copy-start.11 = (bf16[16,1024]{1,0:T(8,128)(2,1)S(1)}, bf16[16,1024]{1,0:T(8,128)(2,1)}, u32[]{:S(2)}) copy-start(bf16[16,1024]{1,0:T(8,128)(2,1)} %up_ref.1) | copy-start | bytes 98308
  38.0 10.8 %copy-start.12 = (bf16[32,128]{1,0:T(8,128)(2,1)S(1)}, bf16[32,128]{1,0:T(8,128)(2,1)}, u32[]{:S(2)}) copy-start(bf16[32,128]{1,0:T(8,128)(2,1)} %kvup_ref.1) | copy-start | bytes 24580
  50.7 16.6 %copy-start.1 = (bf16[512,1024]{1,0:T(8,128)(2,1)S(1)}, bf16[512,1024]{1,0:T(8,128)(2,1)}, u32[]{:S(2)}) copy-start(bf16[512,1024]{1,0:T(8,128)(2,1)} %hidden_ref.3) | copy-start | bytes 3145732
  50.7 16.6 %copy-start.8 = (bf16[512,128]{1,0:T(8,128)(2,1)S(1)}, bf16[512,128]{1,0:T(8,128)(2,1)}, u32[]{:S(2)}) copy-start(bf16[512,128]{1,0:T(8,128)(2,1)} %get-tuple-element.14.key_ref) | copy-start | bytes 393220
  50.7 16.6 %copy-start.9 = (bf16[512,128]{1,0:T(8,128)(2,1)S(1)}, bf16[512,128]{1,0:T(8,128)(2,1)}, u32[]{:S(2)}) copy-start(bf16[512,128]{1,0:T(8,128)(2,1)} %get-tuple-element.15.value_ref) | copy-start | bytes 393220
  67.3 1.2 %copy-start.3 = (bf16[512,1024]{1,0:T(8,128)(2,1)S(1)}, bf16[512,1024]{1,0:T(8,128)(2,1)}, u32[]{:S(2)}) copy-start(bf16[512,1024]{1,0:T(8,128)(2,1)} %get-tuple-element.13.query_ref) | copy-start | bytes 3145732
